TPU v7x, 256 devices: a whole 4x4x8 slice. The times are simulated.
256 devices in a mesh: leaf: 32 (over z, y), front: 8 (over x, core).
Axes of the slice: x: 4, y: 4, z: 8, core: 2. Of those that a mesh axis runs over, the one named last changes fastest.
Arguments:
- leaf_fronts: float32 [32, 1024, 1024], P('leaf', 'front')
- coupling_cols: int32 [32, 8, 124, 128], P('leaf', 'front'), may hold values from 0 to 1023, as said below
- coupling_vals: float32 [32, 8, 124, 128], P('leaf', 'front'), may hold values from -0.1 to 0.1
- sep_diag: float32 [32, 8, 124], P('leaf', 'front'), may hold values from 1 to 3
- child_maps: int32 [62, 512], replicated, may hold values from 0 to 1023, as said below
Outputs:
- factors: float32 [32, 8, 252, 512], P('leaf', 'front')
- log_det: float32 [], replicated
Inputs may be any that keep to these rules, and one draw needn't show every extreme that they name: `coupling_cols`: each coupling column is at most the index, in its front, of the row that holds it, so every entry lies on or below the diagonal. `child_maps`: the 512 entries of each row are distinct.
All inputs are finite; a program needn't handle non-finite values.
Results may differ from a plain program's by a relative error of at most 0.0001.
Values sent between devices are 32-bit elements; how exact they have to be, the bound alone decides.
A program may use at most 128 MiB of HBM per device.

v0:
```python
import functools

import jax
import jax.numpy as jnp
from jax import lax
from jax.experimental import pallas as pl
from jax.experimental.pallas import tpu as pltpu
from jax.sharding import PartitionSpec as P

SEP = 512
BND = 512
WIDE = SEP + BND
NB = 128
F32 = jnp.float32
BF16 = jnp.bfloat16
MESH = pl.DeviceIdType.MESH
VMEM_SPEC = pl.BlockSpec(memory_space=pltpu.VMEM)
SMEM_SPEC = pl.BlockSpec(memory_space=pltpu.SMEM)
HBM_SPEC = pl.BlockSpec(memory_space=pltpu.HBM)
VMEM_LIMIT = 28 * 2**20


def in_hbm(array):
    return pltpu.with_memory_space_constraint(array, pltpu.HBM)


def split2(a):
    hi = a.astype(BF16)
    lo = (a - hi.astype(F32)).astype(BF16)
    return hi, lo


def dg(a, b, ca, cb):
    return lax.dot_general(a, b, (((ca,), (cb,)), ((), ())), preferred_element_type=F32)


def dot3(a, b):
    ah, al = split2(a)
    bh, bl = split2(b)
    return dg(ah, bh, 1, 0) + (dg(ah, bl, 1, 0) + dg(al, bh, 1, 0))


def row_of(x, j):
    return jnp.broadcast_to(x[j : j + 1, :], (8, NB))


def col_of(x, k):
    return jnp.broadcast_to(x[:, k : k + 1], (8, NB))


def diag_factor(dref, nref):
    sub = lax.broadcasted_iota(jnp.int32, (8, NB), 0)
    lane = lax.broadcasted_iota(jnp.int32, (8, NB), 1)
    zero = jnp.zeros((8, NB), F32)
    D = [dref[8 * v : 8 * v + 8, :] for v in range(16)]
    N = [jnp.where(lane == sub + 8 * v, 1.0, 0.0) for v in range(16)]
    for b in range(16):
        cols = [col_of(D[b], 8 * b + k) for k in range(8)]
        a = {(i, k): row_of(cols[k], i) for k in range(8) for i in range(k, 8)}
        drow = [row_of(D[b], j) for j in range(8)]
        nrow = [row_of(N[b], j) for j in range(8)]
        r, l, u, n = {}, {}, [], []
        for j in range(8):
            r[j] = lax.rsqrt(a[j, j])
            for i in range(j + 1, 8):
                l[i, j] = a[i, j] * r[j]
            for k in range(j + 1, 8):
                for i in range(k, 8):
                    a[i, k] = a[i, k] - l[i, j] * l[k, j]
            u.append(drow[j] * r[j])
            n.append(nrow[j] * r[j])
            for i in range(j + 1, 8):
                drow[i] = drow[i] - l[i, j] * u[j]
                nrow[i] = nrow[i] - l[i, j] * n[j]
        for v in range(b + 1, 16):
            c = [col_of(D[v], 8 * b + k) for k in range(8)]
            dv, nv = D[v], N[v]
            for j in range(8):
                lj = c[j] * r[j]
                for k in range(j + 1, 8):
                    c[k] = c[k] - lj * l[k, j]
                dv = dv - lj * u[j]
                nv = nv - lj * n[j]
            D[v], N[v] = dv, nv
        db, nb = u[0], n[0]
        for j in range(1, 8):
            db = jnp.where(sub == j, u[j], db)
            nb = jnp.where(sub == j, n[j], nb)
        D[b] = jnp.where(lane >= 8 * b + sub, db, zero)
        N[b] = nb
        dref[8 * b : 8 * b + 8, :] = D[b]
        nref[8 * b : 8 * b + 8, :] = N[b]


def fac_kernel(level_no, last, offset, size_rows, pos_ref, t_ref, tail_in, *refs):
    if level_no:
        refs = refs[1:]
    out_ref, upd_out, u_ref, d_ref, n_ref, p_ref, piece_ref, tail_ref, upd_ref, sems = refs
    fetch = pltpu.make_async_copy(tail_in, tail_ref, sems.at[0])
    fetch.start()
    u_ref[...] = t_ref[...]
    rows = lax.broadcasted_iota(jnp.int32, (NB, NB), 0)
    cols = lax.broadcasted_iota(jnp.int32, (NB, NB), 1)
    wide = lax.broadcasted_iota(jnp.int32, (NB, WIDE), 1)

    def block(blk, logs):
        o = pl.multiple_of(blk * NB, NB)
        d_ref[...] = u_ref[pl.ds(o, NB), pl.ds(o, NB)]
        diag_factor(d_ref, n_ref)
        d = d_ref[...]
        logs = logs + jnp.sum(jnp.where(rows == cols, jnp.log(d), 0.0).reshape(16, 8, NB), axis=0)
        strip = dot3(n_ref[...], u_ref[pl.ds(o, NB), :])
        strip = jnp.where(wide >= o + NB, strip, 0.0)
        u_ref[pl.ds(o, NB), :] = strip
        u_ref[pl.ds(o, NB), pl.ds(o, NB)] = d
        sh, sl = split2(strip)

        @pl.loop(blk + 1, SEP // NB)
        def trail(jb):
            q = pl.multiple_of(jb * NB, NB)
            lh, ll = split2(u_ref[pl.ds(o, NB), pl.ds(q, NB)].T)
            u_ref[pl.ds(q, NB), :] -= dg(lh, sh, 1, 0) + (dg(lh, sl, 1, 0) + dg(ll, sh, 1, 0))

        return logs

    logs = lax.fori_loop(0, SEP // NB, block, jnp.zeros((8, NB), F32))
    start = pos_ref[level_no]
    base = pl.multiple_of(start // NB * NB, NB)
    p_ref[...] = u_ref[:, pl.ds(base, NB)].T
    if size_rows % 8 == 0:
        piece_ref[...] = p_ref[pl.ds(pl.multiple_of(start - base, 8), size_rows), :]
    else:
        part = start % 8
        block8 = p_ref[pl.ds(pl.multiple_of(start - base - part, 8), 8), :]
        picked = block8[:size_rows]
        for first in range(size_rows, 8, size_rows):
            picked = jnp.where(part == first, block8[first : first + size_rows], picked)
        piece_ref[...] = picked
    store = pltpu.make_async_copy(piece_ref, out_ref.at[offset : offset + size_rows, :], sems.at[1])
    store.start()
    fetch.wait()
    if last:
        upd_out[...] = tail_ref[BND:, :NB] + 2.0 * logs
    else:
        upd_ref[BND:, :NB] = tail_ref[BND:, :NB] + 2.0 * logs
        below = u_ref[:, SEP:]
        bh, bl = split2(below)
        th, tl = split2(below.T)
        moves = []
        for part in range(4):
            at = slice(NB * part, NB * part + NB)
            product = dg(th[at], bh, 1, 0) + (dg(th[at], bl, 1, 0) + dg(tl[at], bh, 1, 0))
            upd_ref[at, :] = tail_ref[at, :] - product
            at = slice(NB * part, NB * part + NB + (8 if part == 3 else 0))
            moves.append(pltpu.make_async_copy(upd_ref.at[at, :], upd_out.at[at, :], sems.at[2 + part]))
            moves[-1].start()
        for move in moves:
            move.wait()
    store.wait()


def factor(level_no, last, offset, size_rows, row_total, pos, t, tail, factors):
    args = [pos, t, in_hbm(tail)] + ([in_hbm(factors)] if level_no else [])
    return pl.pallas_call(
        functools.partial(fac_kernel, level_no, last, offset, size_rows),
        out_shape=[
            pltpu.HBM((row_total, SEP), F32),
            jax.ShapeDtypeStruct((8, NB), F32) if last else pltpu.HBM((BND + 8, BND), F32),
        ],
        in_specs=[SMEM_SPEC, VMEM_SPEC] + [HBM_SPEC] * (len(args) - 2),
        out_specs=[HBM_SPEC, VMEM_SPEC if last else HBM_SPEC],
        scratch_shapes=[
            pltpu.VMEM((SEP, WIDE), F32),
            pltpu.VMEM((NB, NB), F32),
            pltpu.VMEM((NB, NB), F32),
            pltpu.VMEM((NB, SEP), F32),
            pltpu.VMEM((size_rows, SEP), F32),
            pltpu.VMEM((BND + 8, BND), F32),
            pltpu.VMEM((BND + 8, BND), F32),
            pltpu.SemaphoreType.DMA((6,)),
        ],
        input_output_aliases={3: 0} if level_no else {},
        compiler_params=pltpu.CompilerParams(vmem_limit_bytes=VMEM_LIMIT),
    )(*args)


def mirrored(square):
    rows = lax.broadcasted_iota(jnp.int32, square.shape, 0)
    cols = lax.broadcasted_iota(jnp.int32, square.shape, 1)
    return jnp.where(rows >= cols, square, square.T)


def remote(src, dst, send_sem, recv_sem, where):
    return pltpu.make_async_remote_copy(
        src_ref=src, dst_ref=dst, send_sem=send_sem, recv_sem=recv_sem, device_id=where, device_id_type=MESH
    )


def ring_of(count):
    me = lax.axis_index("front")
    chips = count // 2
    chip, core = me // 2, lax.rem(me, 2)
    step = 1 - 2 * core

    def place(offset):
        return lax.rem(chip + offset * step + 2 * chips, chips) * 2 + core

    def twin_of(index):
        return index + 1 - 2 * core

    return me, place, twin_of


def greet(targets):
    barrier = pltpu.get_barrier_semaphore()
    for target in targets:
        pl.semaphore_signal(barrier, inc=1, device_id=target, device_id_type=MESH)
    pl.semaphore_wait(barrier, len(targets))


CUTS = 4
TWIN_SLOT = (1, 0, 2)


def coupling_rows(me, leaf, count, levels, cols_ref, vals_ref, diag_ref, dense_ref, deep_ref):
    sub = lax.broadcasted_iota(jnp.int32, (8, WIDE), 0)
    lane = lax.broadcasted_iota(jnp.int32, (8, WIDE), 1)

    def expand(cols, vals, diag, first_id):
        sums = jnp.where(lane == sub + first_id, jnp.broadcast_to(diag, (8, WIDE)), 0.0)
        for k in range(NB):
            col = jnp.broadcast_to(cols[:, k : k + 1], (8, WIDE))
            val = jnp.broadcast_to(vals[:, k : k + 1], (8, WIDE))
            sums = sums + jnp.where(col == lane, val, 0.0)
        return sums

    def first_row(level_no, local):
        size_rows = WIDE // (count << level_no)
        return (lax.rem(leaf, 1 << level_no) * count + me) * size_rows + local

    rows = cols_ref.shape[0]

    @pl.loop(0, rows // 8)
    def group(g):
        at = pl.ds(pl.multiple_of(g * 8, 8), 8)
        first_id = first_row(1, g * 8)
        for level_no in range(2, levels):
            begin = WIDE // count - 2 * (WIDE // (count << level_no))
            first_id = jnp.where(g * 8 >= begin, first_row(level_no, g * 8 - begin), first_id)
        dense_ref[at, :] = expand(cols_ref[at, :], vals_ref[at, :], diag_ref[at, :], first_id)

    odd = rows % 8
    if odd:
        def tail_of(ref):
            part = ref[rows - odd : rows, :]
            return jnp.concatenate([part] * (8 // odd), axis=0)

        sums = expand(tail_of(cols_ref), tail_of(vals_ref), tail_of(diag_ref), first_row(levels - 1, 0))
        deep_ref[...] = jnp.concatenate([sums[:odd, :SEP], sums[:odd, SEP:]], axis=0)


def level_rows(count, level_no):
    size_rows = WIDE // (count << level_no)
    return size_rows, WIDE // count - 2 * size_rows


def leaf_copies(leaf, count, level_no, dense_ref, deep_ref, pack_ref, deep_land, sems, sending, act):
    span = 1 << level_no
    size_rows, begin = level_rows(count, level_no)
    own = lax.rem(leaf, span)

    @pl.loop(1, span)
    def step(d):
        a = own if sending else lax.rem(own - d + span, span)
        where = {"leaf": leaf - own + (lax.rem(own + d, span) if sending else own)}
        if size_rows % 8:
            act(remote(deep_ref, deep_land.at[a], sems.at[0, 0, d], sems.at[1, 0, d], where))
            return
        left = pl.ds(pl.multiple_of(a * size_rows, size_rows), size_rows)
        src = dense_ref.at[begin : begin + size_rows, :SEP]
        act(remote(src, pack_ref.at[left, :], sems.at[0, 0, d], sems.at[1, 0, d], where))

        @pl.when(a >= span // 2)
        def right_part():
            right = pl.ds(pl.multiple_of(a * size_rows + SEP // count, size_rows), size_rows)
            src = dense_ref.at[begin : begin + size_rows, SEP:]
            act(remote(src, pack_ref.at[right, :], sems.at[0, 1, d], sems.at[1, 1, d], where))


def own_copies(leaf, count, level_no, dense_ref, deep_ref, pack_ref, deep_land, sems, act):
    span = 1 << level_no
    size_rows, begin = level_rows(count, level_no)
    own = lax.rem(leaf, span)
    if size_rows % 8:
        act(pltpu.make_async_copy(deep_ref, deep_land.at[own], sems.at[0, 0, 0]))
        return
    left = pl.ds(pl.multiple_of(own * size_rows, size_rows), size_rows)
    act(pltpu.make_async_copy(dense_ref.at[begin : begin + size_rows, :SEP], pack_ref.at[left, :], sems.at[0, 0, 0]))

    @pl.when(own >= span // 2)
    def right_part():
        right = pl.ds(pl.multiple_of(own * size_rows + SEP // count, size_rows), size_rows)
        src = dense_ref.at[begin : begin + size_rows, SEP:]
        act(pltpu.make_async_copy(src, pack_ref.at[right, :], sems.at[0, 1, 0]))


def start(copy):
    copy.start()


def gather_kernel(
    count, levels, strip_ref, cols_ref, vals_ref, diag_ref, t_ref, tail_out, pack_ref, dense_out, deep_out,
    land_ref, dense_ref, deep_ref, tail_ref, send_sem, recv_sem, leaf_sem, out_sem,
):
    leaf = lax.axis_index("leaf")
    me, place, twin_of = ring_of(count)
    rows = strip_ref.shape[0]
    cut = WIDE // CUTS
    ahead, behind, twin = {"front": place(1)}, {"front": place(-1)}, {"front": twin_of(me)}
    greet([ahead, behind, twin, {"leaf": leaf + 1 - 2 * lax.rem(leaf, 2)}])

    def needed(index, c):
        return index * rows // cut >= c

    def move(slot, index, c, where):
        at = land_ref.at[pl.ds(pl.multiple_of(index * rows, rows), rows), cut * c : cut * c + cut]
        src = strip_ref.at[:, cut * c : cut * c + cut] if slot in (0, 1, 3) else at
        return remote(src, at, send_sem.at[slot, c], recv_sem.at[slot, c], where)

    def each(index, act):
        for c in range(CUTS):
            if c == 0:
                act(c)
            else:
                pl.when(needed(index, c))(functools.partial(act, c))

    each(me, lambda c: move(0, me, c, ahead).start())
    each(me, lambda c: move(1, me, c, behind).start())
    each(me, lambda c: move(3, me, c, twin).start())
    land_ref[pl.ds(pl.multiple_of(me * rows, rows), rows), :] = strip_ref[...]
    coupling_rows(me, leaf, count, levels, cols_ref, vals_ref, diag_ref, dense_ref, deep_ref)
    parts = (leaf, count, 1, dense_ref, deep_ref, pack_ref, None, leaf_sem)
    leaf_copies(*parts, True, start)
    own_copies(*parts, start)
    outs = [
        pltpu.make_async_copy(dense_ref, dense_out, out_sem.at[0]),
        pltpu.make_async_copy(deep_ref, deep_out, out_sem.at[1]),
    ]
    for copy in outs:
        copy.start()
    sources = [place(-1), place(1), place(-2)]

    def arrive(c, k):
        index = sources[k]
        move(k, index, c, ahead).wait_recv()
        if k == 0:
            move(2, index, c, ahead).start()
        move(4 + TWIN_SLOT[k], index, c, twin).start()

    for k in range(3):
        each(sources[k], functools.partial(arrive, k=k))
    for k, index in enumerate([me] + sources):
        each(twin_of(index), lambda c: move(3 + k, twin_of(index), c, twin).wait_recv())
    tail_ref[:BND, :] = mirrored(land_ref[SEP:, SEP:])
    tail_ref[BND:, :] = jnp.zeros((8, BND), F32)
    outs.append(pltpu.make_async_copy(tail_ref, tail_out, out_sem.at[2]))
    outs[-1].start()
    t_ref[:, :SEP] = mirrored(land_ref[:SEP, :SEP])
    t_ref[:, SEP:] = land_ref[SEP:, :SEP].T
    each(me, lambda c: move(3, me, c, twin).wait_send())
    for k, index in enumerate(sources):
        each(index, lambda c: move(4 + TWIN_SLOT[k], index, c, twin).wait_send())
    each(me, lambda c: move(0, me, c, ahead).wait_send())
    each(me, lambda c: move(1, me, c, behind).wait_send())
    each(sources[0], lambda c: move(2, sources[0], c, ahead).wait_send())
    leaf_copies(*parts, False, lambda copy: copy.wait_recv())
    leaf_copies(*parts, True, lambda copy: copy.wait_send())
    own_copies(*parts, lambda copy: copy.wait())
    for copy in outs:
        copy.wait()


def gather_front(strip, cols, vals, diag, count, leaves, cid):
    levels = leaves.bit_length()
    return pl.pallas_call(
        functools.partial(gather_kernel, count, levels),
        out_shape=[
            jax.ShapeDtypeStruct((SEP, WIDE), F32),
            pltpu.HBM((BND + 8, BND), F32),
            pltpu.HBM((3 * SEP // count, SEP), F32),
            pltpu.HBM((WIDE // count, WIDE), F32),
            pltpu.HBM((8, SEP), F32),
        ],
        in_specs=[VMEM_SPEC] * 4,
        out_specs=[VMEM_SPEC] + [HBM_SPEC] * 4,
        scratch_shapes=[
            pltpu.VMEM((WIDE, WIDE), F32),
            pltpu.VMEM((WIDE // count, WIDE), F32),
            pltpu.VMEM((8, SEP), F32),
            pltpu.VMEM((BND + 8, BND), F32),
            pltpu.SemaphoreType.DMA((7, CUTS)),
            pltpu.SemaphoreType.DMA((7, CUTS)),
            pltpu.SemaphoreType.DMA((2, 2, 2)),
            pltpu.SemaphoreType.DMA((3,)),
        ],
        compiler_params=pltpu.CompilerParams(
            collective_id=cid, has_side_effects=True, vmem_limit_bytes=VMEM_LIMIT
        ),
    )(strip, cols, vals, diag)


PART = 32


def chunk_place(index, j):
    first = index // 4 + 1
    if isinstance(index, int):
        return (index, j) if j < first else (15 - index, j - first)
    return jnp.where(j < first, index, 15 - index), jnp.where(j < first, j, j - first)


def pick_of(maps_ref, row):
    ids = lax.broadcasted_iota(jnp.int32, (WIDE, BND), 0)
    return jnp.where(ids == maps_ref[pl.ds(row, 1), :], 1.0, 0.0).astype(BF16)


def swap_kernel(count, bit, map_base, hosts, upd_in, maps_ref, low_in, *refs):
    dense_ref = deep_ref = pack_out = deep_land = None
    if hosts:
        dense_ref, deep_ref, t_ref, tail_out, pack_out, *refs = refs
    else:
        t_ref, tail_out, *refs = refs
    (
        pack_ref, land_ref, sib_ref, nat_ref, natail_ref, ct_ref, ctail_ref, slog_ref, low_ref, tlow_ref,
        upd_ref, tail_ref, log_sem, low_sem, send_sem, recv_sem, *refs,
    ) = refs
    host_level = bit + 2
    span = 1 << host_level if hosts else 2
    odd = hosts and level_rows(count, host_level)[0] % 8 != 0
    fetch = pltpu.make_async_copy(upd_in, upd_ref, low_sem.at[3])
    fetch.start()
    leaf = lax.axis_index("leaf")
    side = lax.rem(leaf // (1 << bit), 2)
    other = {"leaf": leaf + (1 - 2 * side) * (1 << bit)}
    me, place, twin_of = ring_of(count)
    ahead, behind, twin = {"front": place(1)}, {"front": place(-1)}, {"front": twin_of(me)}
    barrier = pltpu.get_barrier_semaphore()
    for target in [ahead, behind, twin] + ([] if hosts else [other]):
        pl.semaphore_signal(barrier, inc=1, device_id=target, device_id_type=MESH)
    if hosts:
        @pl.loop(1, span)
        def greet_leaf(d):
            own = lax.rem(leaf, span)
            where = {"leaf": leaf - own + lax.rem(own + d, span)}
            pl.semaphore_signal(barrier, inc=1, device_id=where, device_id_type=MESH)

        host_sem = refs[0]
        if odd:
            deep_land, gathered_ref = refs[1:]
        parts = (leaf, count, host_level, dense_ref, deep_ref, pack_out, deep_land, host_sem)
        own_copies(*parts, start)
    fetch.wait()
    for j in range(5):
        rb, cb = chunk_place(me, j)
        pack_ref[PART * j : PART * j + PART, :] = upd_ref[
            pl.ds(pl.multiple_of(rb * PART, PART), PART), pl.ds(pl.multiple_of(cb * NB, NB), NB)
        ]
    pl.semaphore_wait(barrier, 3 + span - 1)

    def move(slot, index, where):
        src = pack_ref if slot == 0 else land_ref.at[index]
        return remote(src, land_ref.at[index], send_sem.at[slot], recv_sem.at[slot], where)

    cross = move(0, me, other)
    cross.start()
    logs = remote(upd_ref.at[BND:, :NB], slog_ref, log_sem.at[0], log_sem.at[1], other)
    logs.start()

    twin_low = remote(low_in, tlow_ref, low_sem.at[0], low_sem.at[1], twin)
    twin_low.start()
    own_low = pltpu.make_async_copy(low_in, low_ref, low_sem.at[2])
    own_low.start()
    if hosts:
        leaf_copies(*parts, True, start)
    own_row = map_base + leaf // (1 << bit)
    pick = pick_of(maps_ref, own_row)
    cross.wait_recv()
    sends = [move(1, me, ahead), move(2, me, behind), move(4, me, twin)]
    for copy in sends:
        copy.start()

    uh, ul = split2(upd_ref[:BND, :])
    xh = dg(pick, uh, 1, 0).astype(BF16)
    xl = dg(pick, ul, 1, 0).astype(BF16)
    sources = [place(-1), place(1), place(-2)]
    for k in range(2):
        move(1 + k, sources[k], ahead).wait_recv()
        if k == 0:
            sends.append(move(3, sources[0], ahead))
            sends[-1].start()
        sends.append(move(5 + TWIN_SLOT[k], sources[k], twin))
        sends[-1].start()
    t_ref[...] = dg(xh[:SEP], pick, 1, 1) + dg(xl[:SEP], pick, 1, 1)
    move(3, sources[2], ahead).wait_recv()
    sends.append(move(7, sources[2], twin))
    sends[-1].start()
    tail_ref[:BND, :] = dg(xh[SEP:], pick[SEP:], 1, 1) + dg(xl[SEP:], pick[SEP:], 1, 1)
    own_low.wait()
    twin_low.wait_recv()
    size_rows = WIDE // (count << bit + 1)
    core = lax.rem(me, 2)
    for f in range(count):
        for a in range(2 << bit):
            src, dst = a * size_rows, (a * count + f) * size_rows
            mine = low_ref[f // 2, src : src + size_rows, :]
            other_rows = tlow_ref[f // 2, src : src + size_rows, :]
            nat_ref[dst : dst + size_rows, :] = jnp.where(core == f % 2, mine, other_rows)
            if dst >= SEP:
                src = SEP // count + src
                mine = low_ref[f // 2, src : src + size_rows, :]
                other_rows = tlow_ref[f // 2, src : src + size_rows, :]
                natail_ref[dst - SEP : dst - SEP + size_rows, :] = jnp.where(core == f % 2, mine, other_rows)
    ct_ref[:, :SEP] = mirrored(nat_ref[:SEP, :])
    ct_ref[:, SEP:] = nat_ref[SEP:, :].T
    ctail_ref[...] = mirrored(natail_ref[...])
    pick = pick_of(maps_ref, own_row + 1 - 2 * side)
    logs.wait_recv()
    tail_ref[BND:, :NB] = upd_ref[BND:, :NB] + slog_ref[...]
    for k, index in enumerate([me] + sources):
        move(4 + k, twin_of(index), twin).wait_recv()
    for copy in [cross, logs, twin_low] + sends:
        copy.wait_send()

    for f in range(count):
        for j in range(5):
            rb, cb = chunk_place(f, j)
            sib_ref[rb * PART : rb * PART + PART, cb * NB : cb * NB + NB] = land_ref[f, PART * j : PART * j + PART, :]
    for rb in range(BND // NB):
        for cb in range(rb):
            sib_ref[cb * NB : cb * NB + NB, rb * NB : rb * NB + NB] = sib_ref[
                rb * NB : rb * NB + NB, cb * NB : cb * NB + NB
            ].T
    uh, ul = split2(sib_ref[...])
    xh = dg(pick, uh, 1, 0).astype(BF16)
    xl = dg(pick, ul, 1, 0).astype(BF16)
    tail_ref[:BND, :] = (
        tail_ref[:BND, :] + (dg(xh[SEP:], pick[SEP:], 1, 1) + dg(xl[SEP:], pick[SEP:], 1, 1))
    ) + ctail_ref[...]
    tail_move = pltpu.make_async_copy(tail_ref, tail_out, low_sem.at[4])
    tail_move.start()
    t_ref[...] = (t_ref[...] + (dg(xh[:SEP], pick, 1, 1) + dg(xl[:SEP], pick, 1, 1))) + ct_ref[...]
    if hosts:
        leaf_copies(*parts, False, lambda copy: copy.wait_recv())
        own_copies(*parts, lambda copy: copy.wait())
        if odd:
            size_rows, _ = level_rows(count, host_level)
            for a in range(span):
                gathered_ref[a * size_rows : (a + 1) * size_rows, :] = deep_land[a, :size_rows, :]
                if a >= span // 2:
                    first = SEP // count + a * size_rows
                    gathered_ref[first : first + size_rows, :] = deep_land[a, size_rows : 2 * size_rows, :]
            pack_move = pltpu.make_async_copy(gathered_ref, pack_out, low_sem.at[5])
            pack_move.start()
            pack_move.wait()
        leaf_copies(*parts, True, lambda copy: copy.wait_send())
    tail_move.wait()


def swap_assemble(upd, maps, low, dense, deep, count, bit, map_base, levels, cid):
    hosts = bit + 2 < levels
    args = [in_hbm(upd), maps, in_hbm(low)] + ([in_hbm(dense), in_hbm(deep)] if hosts else [])
    pack_shape = (3 * SEP // count, SEP)
    outs = [jax.ShapeDtypeStruct((SEP, WIDE), F32), pltpu.HBM((BND + 8, BND), F32)]
    scratch = [
        pltpu.VMEM((5 * PART, NB), F32),
        pltpu.VMEM((count, 5 * PART, NB), F32),
        pltpu.VMEM((BND, BND), F32),
        pltpu.VMEM((WIDE, SEP), F32),
        pltpu.VMEM((BND, BND), F32),
        pltpu.VMEM((SEP, WIDE), F32),
        pltpu.VMEM((BND, BND), F32),
        pltpu.VMEM((8, NB), F32),
        pltpu.VMEM((count // 2,) + pack_shape, F32),
        pltpu.VMEM((count // 2,) + pack_shape, F32),
        pltpu.VMEM((BND + 8, BND), F32),
        pltpu.VMEM((BND + 8, BND), F32),
        pltpu.SemaphoreType.DMA((2,)),
        pltpu.SemaphoreType.DMA((6,)),
        pltpu.SemaphoreType.DMA((8,)),
        pltpu.SemaphoreType.DMA((8,)),
    ]
    if hosts:
        span = 4 << bit
        scratch.append(pltpu.SemaphoreType.DMA((2, 2, span)))
        if level_rows(count, bit + 2)[0] % 8:
            scratch += [pltpu.VMEM((span, 8, SEP), F32), pltpu.VMEM(pack_shape, F32)]
    return pl.pallas_call(
        functools.partial(swap_kernel, count, bit, map_base, hosts),
        out_shape=outs + ([pltpu.HBM(pack_shape, F32)] if hosts else []),
        in_specs=[HBM_SPEC, VMEM_SPEC, HBM_SPEC] + [HBM_SPEC] * (len(args) - 3),
        out_specs=[VMEM_SPEC, HBM_SPEC] + [HBM_SPEC] * hosts,
        scratch_shapes=scratch,
        compiler_params=pltpu.CompilerParams(
            collective_id=cid, has_side_effects=True, vmem_limit_bytes=VMEM_LIMIT
        ),
    )(*args)


def body(leaf_fronts, coupling_cols, coupling_vals, sep_diag, child_maps):
    group_count = lax.axis_size("leaf")
    front_count = lax.axis_size("front")
    level_total = group_count.bit_length()
    leaf_pos = lax.axis_index("leaf")
    front_pos = lax.axis_index("front")
    sizes = [WIDE // (front_count << level_no) for level_no in range(level_total)]
    pos = jnp.stack(
        [((leaf_pos & (1 << n) - 1) * front_count + front_pos) * sizes[n] for n in range(level_total)]
    ).astype(jnp.int32)
    same_core = [list(range(core, front_count, 2)) for core in range(2)]
    t, tail, pack, dense, deep = gather_front(
        leaf_fronts[0], coupling_cols[0, 0], coupling_vals[0, 0], sep_diag[0, 0][:, None], front_count, group_count, 0
    )
    factors = None
    map_base = 0
    offset = 0
    for level_no in range(level_total):
        last = level_no + 1 == level_total
        if not last:
            low = lax.all_gather(pack, "front", axis=0, axis_index_groups=same_core)
        factors, upd = factor(level_no, last, offset, sizes[level_no], sum(sizes), pos, t, tail, factors)
        offset += sizes[level_no]
        if last:
            break
        t, tail, *pack = swap_assemble(
            upd, child_maps, low, dense, deep, front_count, level_no, map_base, level_total, 1 + level_no
        )
        pack = pack[0] if pack else None
        map_base += group_count >> level_no
    return (factors[None, None], jnp.sum(upd))


def solution(mesh):
    placed = (
        P("leaf", "front", None),
        P("leaf", "front", None, None),
        P("leaf", "front", None, None),
        P("leaf", "front", None),
        P(),
    )
    return jax.shard_map(
        body,
        mesh=mesh,
        in_specs=placed,
        out_specs=(P("leaf", "front", None, None), P()),
        check_vma=False,
    )
```

profile of v0, /device:TPU:1, one launch (start us, length us, event | category | flops | bytes accessed | tf_op | source)
XLA Modules:
  0.0 328.0 jit_solution(14868190052645250136)
XLA Ops:
  7.2 0.8 copy.19
  8.1 0.8 copy.18
  8.9 0.8 copy.12.diag_ref
  9.7 1.0 copy-done.1
  10.7 24.7 %shard_map.68 = (f32[512,1024]{1,0:T(8,128)S(1)}, f32[520,512]{1,0:T(8,128)}, f32[192,512]{1,0:T(8,128)}, f32[128,1024]{1,0:T(8,128)}, f32[8,512]{1,0:T(8,128)}) custom-call(f32[128,1024]{1,0:T(8,128)S(1)} %bitcast.20, s32[124,128]{1,0:T(8,128)S(1)} %bitcast.21, f32[124,128]{1,0:T(8,128)S(1)} %bitcast.22, f32[124,1]{1,0:T(8,128)S(1)} %copy.12.diag_ref), custom_call_target="tpu_custom_call" | custom-call | tf_op jit(solution)/shard_map/pallas_call | solution.py:385
  35.9 24.2 %shard_map.69 = (f32[252,512]{1,0:T(8,128)}, f32[520,512]{1,0:T(8,128)}) custom-call(s32[6]{0:T(128)S(1)} %stack.27.pos_ref, f32[512,1024]{1,0:T(8,128)S(1)} %get-tuple-element.33.t_ref, f32[520,512]{1,0:T(8,128)} %get-tuple-element.34.tail_in), custom_call_target="tpu_custom_call" | custom-call | tf_op jit(solution)/shard_map/pallas_call | solution.py:164
  60.0 4.5 %all-gather.11.cloned.1.call-done = f32[768,512]{1,0:T(8,128)} async-done(((f32[192,512]{1,0:T(8,128)}), f32[768,512]{1,0:T(8,128)}) %all-gather.11.cloned.1.call-update) | async-done | bytes 1572880 | tf_op jit(solution)/shard_map/all_gather | solution.py:629
  64.5 19.1 %shard_map.70 = (f32[512,1024]{1,0:T(8,128)S(1)}, f32[520,512]{1,0:T(8,128)}, f32[192,512]{1,0:T(8,128)}) custom-call(f32[520,512]{1,0:T(8,128)} %get-tuple-element.35.upd_in, s32[62,512]{1,0:T(8,128)S(1)} %copy-done, f32[4,192,512]{2,1,0:T(8,128)} %bitcast.24, f32[128,1024]{1,0:T(8,128)} %get-tuple-element.37.refs_0_, f32[8,512]{1,0:T(8,128)} %get-tuple-element.38.refs_1_), custom_call_target="tpu_custom_call" | custom-call | tf_op jit(solution)/shard_map/pallas_call | solution.py:597
  83.7 0.6 all-gather.15.cloned.1.call-start
  84.2 24.1 %shard_map.71 = (f32[252,512]{1,0:T(8,128)}, f32[520,512]{1,0:T(8,128)}) custom-call(s32[6]{0:T(128)S(1)} %stack.27.pos_ref, f32[512,1024]{1,0:T(8,128)S(1)} %get-tuple-element.39.t_ref, f32[520,512]{1,0:T(8,128)} %get-tuple-element.40.tail_in, f32[252,512]{1,0:T(8,128)} %get-tuple-element.41.refs_0_), custom_call_target="tpu_custom_call", output_to_operand_aliasing={{0}: (3, {})} | custom-call | tf_op jit(solution)/shard_map/pallas_call | solution.py:164
  108.4 3.9 %all-gather.13.cloned.1.call-done = f32[768,512]{1,0:T(8,128)} async-done(((f32[192,512]{1,0:T(8,128)}), f32[768,512]{1,0:T(8,128)}) %all-gather.13.cloned.1.call-update) | async-done | bytes 1572880 | tf_op jit(solution)/shard_map/all_gather | solution.py:629
  112.3 23.0 %shard_map.72 = (f32[512,1024]{1,0:T(8,128)S(1)}, f32[520,512]{1,0:T(8,128)}, f32[192,512]{1,0:T(8,128)}) custom-call(f32[520,512]{1,0:T(8,128)} %get-tuple-element.42.upd_in, s32[62,512]{1,0:T(8,128)S(1)} %copy-done, f32[4,192,512]{2,1,0:T(8,128)} %bitcast.26, f32[128,1024]{1,0:T(8,128)} %get-tuple-element.37.refs_0_, f32[8,512]{1,0:T(8,128)} %get-tuple-element.38.refs_1_), custom_call_target="tpu_custom_call" | custom-call | tf_op jit(solution)/shard_map/pallas_call | solution.py:597
  135.6 24.1 %shard_map.73 = (f32[252,512]{1,0:T(8,128)}, f32[520,512]{1,0:T(8,128)}) custom-call(s32[6]{0:T(128)S(1)} %stack.27.pos_ref, f32[512,1024]{1,0:T(8,128)S(1)} %get-tuple-element.44.t_ref, f32[520,512]{1,0:T(8,128)} %get-tuple-element.45.tail_in, f32[252,512]{1,0:T(8,128)} %get-tuple-element.46.refs_0_), custom_call_target="tpu_custom_call", output_to_operand_aliasing={{0}: (3, {})} | custom-call | tf_op jit(solution)/shard_map/pallas_call | solution.py:164
  159.7 2.6 all-gather.15.cloned.1.call-done
  162.3 26.9 %shard_map.74 = (f32[512,1024]{1,0:T(8,128)S(1)}, f32[520,512]{1,0:T(8,128)}, f32[192,512]{1,0:T(8,128)}) custom-call(f32[520,512]{1,0:T(8,128)} %get-tuple-element.47.upd_in, s32[62,512]{1,0:T(8,128)S(1)} %copy-done, f32[4,192,512]{2,1,0:T(8,128)} %bitcast.27, f32[128,1024]{1,0:T(8,128)} %get-tuple-element.37.refs_0_, f32[8,512]{1,0:T(8,128)} %get-tuple-element.38.refs_1_), custom_call_target="tpu_custom_call" | custom-call | tf_op jit(solution)/shard_map/pallas_call | solution.py:597
  189.5 24.1 %shard_map.75 = (f32[252,512]{1,0:T(8,128)}, f32[520,512]{1,0:T(8,128)}) custom-call(s32[6]{0:T(128)S(1)} %stack.27.pos_ref, f32[512,1024]{1,0:T(8,128)S(1)} %get-tuple-element.49.t_ref, f32[520,512]{1,0:T(8,128)} %get-tuple-element.50.tail_in, f32[252,512]{1,0:T(8,128)} %get-tuple-element.51.refs_0_), custom_call_target="tpu_custom_call", output_to_operand_aliasing={{0}: (3, {})} | custom-call | tf_op jit(solution)/shard_map/pallas_call | solution.py:164
  213.7 1.0 all-gather.17.cloned.1.call-done
  214.7 31.0 %shard_map.76 = (f32[512,1024]{1,0:T(8,128)S(1)}, f32[520,512]{1,0:T(8,128)}, f32[192,512]{1,0:T(8,128)}) custom-call(f32[520,512]{1,0:T(8,128)} %get-tuple-element.52.upd_in, s32[62,512]{1,0:T(8,128)S(1)} %copy-done, f32[4,192,512]{2,1,0:T(8,128)} %bitcast.25, f32[128,1024]{1,0:T(8,128)} %get-tuple-element.37.refs_0_, f32[8,512]{1,0:T(8,128)} %get-tuple-element.38.refs_1_), custom_call_target="tpu_custom_call" | custom-call | tf_op jit(solution)/shard_map/pallas_call | solution.py:597
  245.7 24.5 %shard_map.77 = (f32[252,512]{1,0:T(8,128)}, f32[520,512]{1,0:T(8,128)}) custom-call(s32[6]{0:T(128)S(1)} %stack.27.pos_ref, f32[512,1024]{1,0:T(8,128)S(1)} %get-tuple-element.54.t_ref, f32[520,512]{1,0:T(8,128)} %get-tuple-element.55.tail_in, f32[252,512]{1,0:T(8,128)} %get-tuple-element.56.refs_0_), custom_call_target="tpu_custom_call", output_to_operand_aliasing={{0}: (3, {})} | custom-call | tf_op jit(solution)/shard_map/pallas_call | solution.py:164
  270.2 2.2 all-gather.19.cloned.1.call-done
  272.5 22.7 %shard_map.78 = (f32[512,1024]{1,0:T(8,128)S(1)}, f32[520,512]{1,0:T(8,128)}) custom-call(f32[520,512]{1,0:T(8,128)} %get-tuple-element.57.upd_in, s32[62,512]{1,0:T(8,128)S(1)} %copy-done, f32[4,192,512]{2,1,0:T(8,128)} %bitcast.28), custom_call_target="tpu_custom_call" | custom-call | tf_op jit(solution)/shard_map/pallas_call | solution.py:597
  295.2 23.1 %shard_map.79 = (f32[252,512]{1,0:T(8,128)}, f32[8,128]{1,0:T(8,128)S(1)}) custom-call(s32[6]{0:T(128)S(1)} %stack.27.pos_ref, f32[512,1024]{1,0:T(8,128)S(1)} %get-tuple-element.59.t_ref, f32[520,512]{1,0:T(8,128)} %get-tuple-element.60.tail_in, f32[252,512]{1,0:T(8,128)} %get-tuple-element.61.refs_0_), custom_call_target="tpu_custom_call", output_to_operand_aliasing={{0}: (3, {})} | custom-call | tf_op jit(solution)/shard_map/pallas_call | solution.py:164
  318.4 2.4 copy.13
  320.7 0.6 reduce_sum.9
  (13 shorter events, 1.0 us)
Async XLA Ops:
  7.2 57.4 %all-gather.11.cloned.1.call-start = ((), (), s32[]{:S(2)}) async-start(), calls=%async_computation | async-start | bytes 1966080 | tf_op jit(solution)/shard_map/all_gather | solution.py:629
  9.7 1.0 copy-start.1
  35.4 76.9 %all-gather.13.cloned.1.call-start = ((), (), s32[]{:S(2)}) async-start(), calls=%async_computation.1 | async-start | bytes 1966080 | tf_op jit(solution)/shard_map/all_gather | solution.py:629
  35.9 28.7 %copy-start = (s32[62,512]{1,0:T(8,128)S(1)}, s32[62,512]{1,0:T(8,128)}, u32[]{:S(2)}) copy-start(s32[62,512]{1,0:T(8,128)} %maps_ref.9) | copy-start | bytes 380932
  83.7 78.7 %all-gather.15.cloned.1.call-start = ((), (), s32[]{:S(2)}) async-start(), calls=%async_computation.2 | async-start | bytes 1966080 | tf_op jit(solution)/shard_map/all_gather | solution.py:629
  135.4 79.3 %all-gather.17.cloned.1.call-start = ((), (), s32[]{:S(2)}) async-start(), calls=%async_computation.3 | async-start | bytes 1966080 | tf_op jit(solution)/shard_map/all_gather | solution.py:629
  189.3 83.2 %all-gather.19.cloned.1.call-start = ((), (), s32[]{:S(2)}) async-start(), calls=%async_computation.4 | async-start | bytes 1966080 | tf_op jit(solution)/shard_map/all_gather | solution.py:629
Sparse Core Ops, SparseCore 0:
  35.6 28.9 all-gather.10
  83.8 28.4 all-gather.12
  135.5 26.7 all-gather.14
  189.4 25.2 all-gather.16
  245.8 26.6 all-gather.18
where the time goes:
time: 331 us; the launch traced here: 328 us
  Pallas kernels  292 us (88%)
  waiting for transfers between devices  14.4 us (4%)
  between operations  14.1 us (4%)
  local copies, waits for them, and re-layouts  5.94 us (2%)
    pallas_call x6, Pallas kernels, factor(): pl.pallas_call(functools.partial(fac_kernel, level_no, last, offset, size...  144 us
    pallas_call x5, Pallas kernels, swap_assemble(): pl.pallas_call(functools.partial(swap_kernel, count, bit, map_base, hosts...  123 us
    pallas_call x1, Pallas kernels, gather_front(): pl.pallas_call(functools.partial(gather_kernel, count, levels), out_shape...  24.7 us
    all_gather x5, waiting for transfers between devices, body(): low = lax.all_gather(pack, 'front', axis=0, axis_index_groups=same_core)  14.3 us
  transfers between devices with their start and end apart: 5, of which 5 were waited for; matrix products, arithmetic and copies ran while one was open for 0% of the time, Pallas kernels for 37%

commit v1 on v0

--- a/solution.py
+++ b/solution.py
@@ -55,7 +55,9 @@
     D = [dref[8 * v : 8 * v + 8, :] for v in range(16)]
     N = [jnp.where(lane == sub + 8 * v, 1.0, 0.0) for v in range(16)]
     for b in range(16):
-        cols = [col_of(D[b], 8 * b + k) for k in range(8)]
+        cols = ahead if b else [col_of(D[0], k) for k in range(8)]
+        if b < 15:
+            ahead = [col_of(D[b + 1], 8 * b + 8 + k) for k in range(8)]
         a = {(i, k): row_of(cols[k], i) for k in range(8) for i in range(k, 8)}
         drow = [row_of(D[b], j) for j in range(8)]
         nrow = [row_of(N[b], j) for j in range(8)]
@@ -79,6 +81,8 @@
                 lj = c[j] * r[j]
                 for k in range(j + 1, 8):
                     c[k] = c[k] - lj * l[k, j]
+                if v == b + 1:
+                    ahead = [ahead[k] - lj * row_of(lj, k) for k in range(8)]
                 dv = dv - lj * u[j]
                 nv = nv - lj * n[j]
             D[v], N[v] = dv, nv
@@ -309,15 +313,29 @@
 
 
 def gather_kernel(
-    count, levels, strip_ref, cols_ref, vals_ref, diag_ref, t_ref, tail_out, pack_ref, dense_out, deep_out,
-    land_ref, dense_ref, deep_ref, tail_ref, send_sem, recv_sem, leaf_sem, out_sem,
+    count, levels, hosted, strip_in, cols_in, vals_in, diag_ref, t_ref, tail_out, *refs
 ):
+    packs = refs[:hosted]
+    (
+        dense_out, deep_out, land_ref, dense_ref, deep_ref, tail_ref, strip_ref, cols_ref, vals_ref,
+        send_sem, recv_sem, out_sem, *leaf_sems,
+    ) = refs[hosted:]
+    fetches = [
+        pltpu.make_async_copy(strip_in, strip_ref, out_sem.at[3]),
+        pltpu.make_async_copy(cols_in, cols_ref, out_sem.at[4]),
+        pltpu.make_async_copy(vals_in, vals_ref, out_sem.at[5]),
+    ]
+    for copy in fetches:
+        copy.start()
     leaf = lax.axis_index("leaf")
     me, place, twin_of = ring_of(count)
     rows = strip_ref.shape[0]
     cut = WIDE // CUTS
     ahead, behind, twin = {"front": place(1)}, {"front": place(-1)}, {"front": twin_of(me)}
-    greet([ahead, behind, twin, {"leaf": leaf + 1 - 2 * lax.rem(leaf, 2)}])
+    span = 1 << hosted
+    others = [{"leaf": leaf - lax.rem(leaf, span) + lax.rem(leaf + d, span)} for d in range(1, span)]
+    greet([ahead, behind, twin] + others)
+    fetches[0].wait()
 
     def needed(index, c):
         return index * rows // cut >= c
@@ -338,10 +356,13 @@
     each(me, lambda c: move(1, me, c, behind).start())
     each(me, lambda c: move(3, me, c, twin).start())
     land_ref[pl.ds(pl.multiple_of(me * rows, rows), rows), :] = strip_ref[...]
+    for copy in fetches[1:]:
+        copy.wait()
     coupling_rows(me, leaf, count, levels, cols_ref, vals_ref, diag_ref, dense_ref, deep_ref)
-    parts = (leaf, count, 1, dense_ref, deep_ref, pack_ref, None, leaf_sem)
-    leaf_copies(*parts, True, start)
-    own_copies(*parts, start)
+    parts = [(leaf, count, n + 1, dense_ref, deep_ref, packs[n], None, leaf_sems[n]) for n in range(hosted)]
+    for part in parts:
+        leaf_copies(*part, True, start)
+        own_copies(*part, start)
     outs = [
         pltpu.make_async_copy(dense_ref, dense_out, out_sem.at[0]),
         pltpu.make_async_copy(deep_ref, deep_out, out_sem.at[1]),
@@ -373,40 +394,45 @@
     each(me, lambda c: move(0, me, c, ahead).wait_send())
     each(me, lambda c: move(1, me, c, behind).wait_send())
     each(sources[0], lambda c: move(2, sources[0], c, ahead).wait_send())
-    leaf_copies(*parts, False, lambda copy: copy.wait_recv())
-    leaf_copies(*parts, True, lambda copy: copy.wait_send())
-    own_copies(*parts, lambda copy: copy.wait())
+    for part in parts:
+        leaf_copies(*part, False, lambda copy: copy.wait_recv())
+        leaf_copies(*part, True, lambda copy: copy.wait_send())
+        own_copies(*part, lambda copy: copy.wait())
     for copy in outs:
         copy.wait()
 
 
 def gather_front(strip, cols, vals, diag, count, leaves, cid):
     levels = leaves.bit_length()
+    hosted = min(2, levels - 1)
     return pl.pallas_call(
-        functools.partial(gather_kernel, count, levels),
+        functools.partial(gather_kernel, count, levels, hosted),
         out_shape=[
             jax.ShapeDtypeStruct((SEP, WIDE), F32),
             pltpu.HBM((BND + 8, BND), F32),
-            pltpu.HBM((3 * SEP // count, SEP), F32),
+            *[pltpu.HBM((3 * SEP // count, SEP), F32)] * hosted,
             pltpu.HBM((WIDE // count, WIDE), F32),
             pltpu.HBM((8, SEP), F32),
         ],
-        in_specs=[VMEM_SPEC] * 4,
-        out_specs=[VMEM_SPEC] + [HBM_SPEC] * 4,
+        in_specs=[HBM_SPEC] * 3 + [VMEM_SPEC],
+        out_specs=[VMEM_SPEC] + [HBM_SPEC] * (3 + hosted),
         scratch_shapes=[
             pltpu.VMEM((WIDE, WIDE), F32),
             pltpu.VMEM((WIDE // count, WIDE), F32),
             pltpu.VMEM((8, SEP), F32),
             pltpu.VMEM((BND + 8, BND), F32),
+            pltpu.VMEM(strip.shape, F32),
+            pltpu.VMEM(cols.shape, jnp.int32),
+            pltpu.VMEM(vals.shape, F32),
             pltpu.SemaphoreType.DMA((7, CUTS)),
             pltpu.SemaphoreType.DMA((7, CUTS)),
-            pltpu.SemaphoreType.DMA((2, 2, 2)),
-            pltpu.SemaphoreType.DMA((3,)),
-        ],
+            pltpu.SemaphoreType.DMA((6,)),
+        ]
+        + [pltpu.SemaphoreType.DMA((2, 2, 2 << n)) for n in range(hosted)],
         compiler_params=pltpu.CompilerParams(
             collective_id=cid, has_side_effects=True, vmem_limit_bytes=VMEM_LIMIT
         ),
-    )(strip, cols, vals, diag)
+    )(in_hbm(strip), in_hbm(cols), in_hbm(vals), diag)
 
 
 PART = 32
@@ -434,7 +460,7 @@
         pack_ref, land_ref, sib_ref, nat_ref, natail_ref, ct_ref, ctail_ref, slog_ref, low_ref, tlow_ref,
         upd_ref, tail_ref, log_sem, low_sem, send_sem, recv_sem, *refs,
     ) = refs
-    host_level = bit + 2
+    host_level = bit + 3
     span = 1 << host_level if hosts else 2
     odd = hosts and level_rows(count, host_level)[0] % 8 != 0
     fetch = pltpu.make_async_copy(upd_in, upd_ref, low_sem.at[3])
@@ -567,7 +593,7 @@
 
 
 def swap_assemble(upd, maps, low, dense, deep, count, bit, map_base, levels, cid):
-    hosts = bit + 2 < levels
+    hosts = bit + 3 < levels
     args = [in_hbm(upd), maps, in_hbm(low)] + ([in_hbm(dense), in_hbm(deep)] if hosts else [])
     pack_shape = (3 * SEP // count, SEP)
     outs = [jax.ShapeDtypeStruct((SEP, WIDE), F32), pltpu.HBM((BND + 8, BND), F32)]
@@ -590,9 +616,9 @@
         pltpu.SemaphoreType.DMA((8,)),
     ]
     if hosts:
-        span = 4 << bit
+        span = 8 << bit
         scratch.append(pltpu.SemaphoreType.DMA((2, 2, span)))
-        if level_rows(count, bit + 2)[0] % 8:
+        if level_rows(count, bit + 3)[0] % 8:
             scratch += [pltpu.VMEM((span, 8, SEP), F32), pltpu.VMEM(pack_shape, F32)]
     return pl.pallas_call(
         functools.partial(swap_kernel, count, bit, map_base, hosts),
@@ -617,7 +643,7 @@
         [((leaf_pos & (1 << n) - 1) * front_count + front_pos) * sizes[n] for n in range(level_total)]
     ).astype(jnp.int32)
     same_core = [list(range(core, front_count, 2)) for core in range(2)]
-    t, tail, pack, dense, deep = gather_front(
+    t, tail, *packs, dense, deep = gather_front(
         leaf_fronts[0], coupling_cols[0, 0], coupling_vals[0, 0], sep_diag[0, 0][:, None], front_count, group_count, 0
     )
     factors = None
@@ -626,15 +652,15 @@
     for level_no in range(level_total):
         last = level_no + 1 == level_total
         if not last:
-            low = lax.all_gather(pack, "front", axis=0, axis_index_groups=same_core)
+            low = lax.all_gather(packs[level_no], "front", axis=0, axis_index_groups=same_core)
         factors, upd = factor(level_no, last, offset, sizes[level_no], sum(sizes), pos, t, tail, factors)
         offset += sizes[level_no]
         if last:
             break
-        t, tail, *pack = swap_assemble(
+        t, tail, *more = swap_assemble(
             upd, child_maps, low, dense, deep, front_count, level_no, map_base, level_total, 1 + level_no
         )
-        pack = pack[0] if pack else None
+        packs += more
         map_base += group_count >> level_no
     return (factors[None, None], jnp.sum(upd))
 

time: 331 us -> 295 us (0.89)
  Pallas kernels: 292 us -> 260 us
  waiting for transfers between devices: 14.4 us -> 10 us
    pallas_call x6, Pallas kernels: 144 us -> 116 us  [factor(): pl.pallas_call(functools.partial(fac_kernel, level_no, last, offset, size...]
    all_gather x5, waiting for transfers between devices: 14.3 us -> 9.28 us  [body(): lax.all_gather(packs[level_no], 'front', axis=0, axis_index_groups=same_c...]
    pallas_call x5, Pallas kernels: 123 us -> 118 us  [swap_assemble(): pl.pallas_call(functools.partial(swap_kernel, count, bit, map_base, hosts...]
  transfers between devices with their start and end apart: 5 -> 5, of which waited for: 5 -> 1; matrix products, arithmetic and copies ran while one was open for 0% -> 0% of each run, Pallas kernels for 37% -> 66%
where the time goes in v1:
time: 295 us; the launch traced here: 292 us
  Pallas kernels  260 us (88%)
  between operations  14.1 us (5%)
  waiting for transfers between devices  10 us (3%)
  local copies, waits for them, and re-layouts  6.14 us (2%)
    pallas_call x5, Pallas kernels, swap_assemble(): pl.pallas_call(functools.partial(swap_kernel, count, bit, map_base, hosts...  118 us
    pallas_call x6, Pallas kernels, factor(): pl.pallas_call(functools.partial(fac_kernel, level_no, last, offset, size...  116 us
    pallas_call x1, Pallas kernels, gather_front(): pl.pallas_call(functools.partial(gather_kernel, count, levels, hosted), o...  26.5 us
    all_gather x5, waiting for transfers between devices, body(): lax.all_gather(packs[level_no], 'front', axis=0, axis_index_groups=same_c...  9.28 us
  transfers between devices with their start and end apart: 5, of which 1 were waited for; matrix products, arithmetic and copies ran while one was open for 0% of the time, Pallas kernels for 66%

profile of v1, /device:TPU:1, one launch (start us, length us, event | category | flops | bytes accessed | tf_op | source)
XLA Modules:
  0.0 292.2 jit_solution(2528707314293540910)
XLA Ops:
  7.2 1.5 copy.18
  8.7 1.5 copy.19
  10.1 0.8 copy.12.diag_ref
  10.9 26.5 %shard_map.68 = (f32[512,1024]{1,0:T(8,128)S(1)}, f32[520,512]{1,0:T(8,128)}, f32[192,512]{1,0:T(8,128)}, f32[192,512]{1,0:T(8,128)}, f32[128,1024]{1,0:T(8,128)}, /*index=5*/f32[8,512]{1,0:T(8,128)}) custom-call(f32[128,1024]{1,0:T(8,128)} %bitcast.26, s32[124,128]{1,0:T(8,128)} %bitcast.28, f32[124,128]{1,0:T(8,128)} %bitcast.27, f32[124,1]{1,0:T(8,128)S(1)} %copy.12.diag_ref), custom_call_target="tpu_custom_call" | custom-call | tf_op jit(solution)/shard_map/pallas_call | solution.py:408
  37.5 0.0 all-gather.13.cloned.1.call-start
  37.5 0.7 all-gather.13.cloned.1.call-update
  38.2 0.3 all-gather.15.cloned.1.call-start
  38.6 0.1 stack.27.pos_ref
  38.6 19.4 %shard_map.69 = (f32[252,512]{1,0:T(8,128)}, f32[520,512]{1,0:T(8,128)}) custom-call(s32[6]{0:T(128)S(1)} %stack.27.pos_ref, f32[512,1024]{1,0:T(8,128)S(1)} %get-tuple-element.33.t_ref, f32[520,512]{1,0:T(8,128)} %get-tuple-element.34.tail_in), custom_call_target="tpu_custom_call" | custom-call | tf_op jit(solution)/shard_map/pallas_call | solution.py:168
  58.0 9.2 %all-gather.11.cloned.1.call-done = f32[768,512]{1,0:T(8,128)} async-done(((f32[192,512]{1,0:T(8,128)}), f32[768,512]{1,0:T(8,128)}) %all-gather.11.cloned.1.call-update) | async-done | bytes 1572880 | tf_op jit(solution)/shard_map/all_gather | solution.py:655
  67.2 21.7 %shard_map.70 = (f32[512,1024]{1,0:T(8,128)S(1)}, f32[520,512]{1,0:T(8,128)}, f32[192,512]{1,0:T(8,128)}) custom-call(f32[520,512]{1,0:T(8,128)} %get-tuple-element.35.upd_in, s32[62,512]{1,0:T(8,128)S(1)} %copy-done, f32[4,192,512]{2,1,0:T(8,128)} %bitcast.22, f32[128,1024]{1,0:T(8,128)} %get-tuple-element.37.refs_0_, f32[8,512]{1,0:T(8,128)} %get-tuple-element.38.refs_1_), custom_call_target="tpu_custom_call" | custom-call | tf_op jit(solution)/shard_map/pallas_call | solution.py:623
  88.9 0.6 all-gather.17.cloned.1.call-start
  89.5 19.3 %shard_map.71 = (f32[252,512]{1,0:T(8,128)}, f32[520,512]{1,0:T(8,128)}) custom-call(s32[6]{0:T(128)S(1)} %stack.27.pos_ref, f32[512,1024]{1,0:T(8,128)S(1)} %get-tuple-element.39.t_ref, f32[520,512]{1,0:T(8,128)} %get-tuple-element.40.tail_in, f32[252,512]{1,0:T(8,128)} %get-tuple-element.41.refs_0_), custom_call_target="tpu_custom_call", output_to_operand_aliasing={{0}: (3, {})} | custom-call | tf_op jit(solution)/shard_map/pallas_call | solution.py:168
  108.9 28.5 %shard_map.72 = (f32[512,1024]{1,0:T(8,128)S(1)}, f32[520,512]{1,0:T(8,128)}, f32[192,512]{1,0:T(8,128)}) custom-call(f32[520,512]{1,0:T(8,128)} %get-tuple-element.42.upd_in, s32[62,512]{1,0:T(8,128)S(1)} %copy-done, f32[4,192,512]{2,1,0:T(8,128)} %bitcast.21, f32[128,1024]{1,0:T(8,128)} %get-tuple-element.37.refs_0_, f32[8,512]{1,0:T(8,128)} %get-tuple-element.38.refs_1_), custom_call_target="tpu_custom_call" | custom-call | tf_op jit(solution)/shard_map/pallas_call | solution.py:623
  137.4 0.2 all-gather.19.cloned.1.call-start
  137.6 19.3 %shard_map.73 = (f32[252,512]{1,0:T(8,128)}, f32[520,512]{1,0:T(8,128)}) custom-call(s32[6]{0:T(128)S(1)} %stack.27.pos_ref, f32[512,1024]{1,0:T(8,128)S(1)} %get-tuple-element.44.t_ref, f32[520,512]{1,0:T(8,128)} %get-tuple-element.45.tail_in, f32[252,512]{1,0:T(8,128)} %get-tuple-element.46.refs_0_), custom_call_target="tpu_custom_call", output_to_operand_aliasing={{0}: (3, {})} | custom-call | tf_op jit(solution)/shard_map/pallas_call | solution.py:168
  157.0 23.1 %shard_map.74 = (f32[512,1024]{1,0:T(8,128)S(1)}, f32[520,512]{1,0:T(8,128)}, f32[192,512]{1,0:T(8,128)}) custom-call(f32[520,512]{1,0:T(8,128)} %get-tuple-element.47.upd_in, s32[62,512]{1,0:T(8,128)S(1)} %copy-done, f32[4,192,512]{2,1,0:T(8,128)} %bitcast.23, f32[128,1024]{1,0:T(8,128)} %get-tuple-element.37.refs_0_, f32[8,512]{1,0:T(8,128)} %get-tuple-element.38.refs_1_), custom_call_target="tpu_custom_call" | custom-call | tf_op jit(solution)/shard_map/pallas_call | solution.py:623
  180.1 19.5 %shard_map.75 = (f32[252,512]{1,0:T(8,128)}, f32[520,512]{1,0:T(8,128)}) custom-call(s32[6]{0:T(128)S(1)} %stack.27.pos_ref, f32[512,1024]{1,0:T(8,128)S(1)} %get-tuple-element.49.t_ref, f32[520,512]{1,0:T(8,128)} %get-tuple-element.50.tail_in, f32[252,512]{1,0:T(8,128)} %get-tuple-element.51.refs_0_), custom_call_target="tpu_custom_call", output_to_operand_aliasing={{0}: (3, {})} | custom-call | tf_op jit(solution)/shard_map/pallas_call | solution.py:168
  199.7 23.2 %shard_map.76 = (f32[512,1024]{1,0:T(8,128)S(1)}, f32[520,512]{1,0:T(8,128)}) custom-call(f32[520,512]{1,0:T(8,128)} %get-tuple-element.52.upd_in, s32[62,512]{1,0:T(8,128)S(1)} %copy-done, f32[4,192,512]{2,1,0:T(8,128)} %bitcast.24), custom_call_target="tpu_custom_call" | custom-call | tf_op jit(solution)/shard_map/pallas_call | solution.py:623
  222.9 19.7 %shard_map.77 = (f32[252,512]{1,0:T(8,128)}, f32[520,512]{1,0:T(8,128)}) custom-call(s32[6]{0:T(128)S(1)} %stack.27.pos_ref, f32[512,1024]{1,0:T(8,128)S(1)} %get-tuple-element.54.t_ref, f32[520,512]{1,0:T(8,128)} %get-tuple-element.55.tail_in, f32[252,512]{1,0:T(8,128)} %get-tuple-element.56.refs_0_), custom_call_target="tpu_custom_call", output_to_operand_aliasing={{0}: (3, {})} | custom-call | tf_op jit(solution)/shard_map/pallas_call | solution.py:168
  242.7 21.5 %shard_map.78 = (f32[512,1024]{1,0:T(8,128)S(1)}, f32[520,512]{1,0:T(8,128)}) custom-call(f32[520,512]{1,0:T(8,128)} %get-tuple-element.57.upd_in, s32[62,512]{1,0:T(8,128)S(1)} %copy-done, f32[4,192,512]{2,1,0:T(8,128)} %bitcast.25), custom_call_target="tpu_custom_call" | custom-call | tf_op jit(solution)/shard_map/pallas_call | solution.py:623
  264.2 18.3 %shard_map.79 = (f32[252,512]{1,0:T(8,128)}, f32[8,128]{1,0:T(8,128)S(1)}) custom-call(s32[6]{0:T(128)S(1)} %stack.27.pos_ref, f32[512,1024]{1,0:T(8,128)S(1)} %get-tuple-element.59.t_ref, f32[520,512]{1,0:T(8,128)} %get-tuple-element.60.tail_in, f32[252,512]{1,0:T(8,128)} %get-tuple-element.61.refs_0_), custom_call_target="tpu_custom_call", output_to_operand_aliasing={{0}: (3, {})} | custom-call | tf_op jit(solution)/shard_map/pallas_call | solution.py:168
  282.5 2.4 copy.13
  284.8 0.6 reduce_sum.9
  (11 shorter events, 0.2 us)
Async XLA Ops:
  7.2 60.0 %all-gather.11.cloned.1.call-start = ((), (), s32[]{:S(2)}) async-start(), calls=%async_computation | async-start | bytes 1966080 | tf_op jit(solution)/shard_map/all_gather | solution.py:655
  37.5 71.4 %all-gather.13.cloned.1.call-start = ((), (), s32[]{:S(2)}) async-start(), calls=%async_computation.1 | async-start | bytes 1966080 | tf_op jit(solution)/shard_map/all_gather | solution.py:655
  38.2 118.8 %all-gather.15.cloned.1.call-start = ((), (), s32[]{:S(2)}) async-start(), calls=%async_computation.2 | async-start | bytes 1966080 | tf_op jit(solution)/shard_map/all_gather | solution.py:655
  38.6 28.6 %copy-start = (s32[62,512]{1,0:T(8,128)S(1)}, s32[62,512]{1,0:T(8,128)}, u32[]{:S(2)}) copy-start(s32[62,512]{1,0:T(8,128)} %maps_ref.9) | copy-start | bytes 380932
  88.9 110.7 %all-gather.17.cloned.1.call-start = ((), (), s32[]{:S(2)}) async-start(), calls=%async_computation.3 | async-start | bytes 1966080 | tf_op jit(solution)/shard_map/all_gather | solution.py:655
  137.4 105.3 %all-gather.19.cloned.1.call-start = ((), (), s32[]{:S(2)}) async-start(), calls=%async_computation.4 | async-start | bytes 1966080 | tf_op jit(solution)/shard_map/all_gather | solution.py:655
Sparse Core Ops, SparseCore 0:
  37.6 29.5 all-gather.10
  69.0 29.1 all-gather.12
  100.0 31.1 all-gather.14
  137.5 24.2 all-gather.16
  180.2 28.4 all-gather.18

commit v2 on v1

--- a/solution.py
+++ b/solution.py
@@ -53,14 +53,16 @@
     lane = lax.broadcasted_iota(jnp.int32, (8, NB), 1)
     zero = jnp.zeros((8, NB), F32)
     D = [dref[8 * v : 8 * v + 8, :] for v in range(16)]
-    N = [jnp.where(lane == sub + 8 * v, 1.0, 0.0) for v in range(16)]
     for b in range(16):
         cols = ahead if b else [col_of(D[0], k) for k in range(8)]
         if b < 15:
             ahead = [col_of(D[b + 1], 8 * b + 8 + k) for k in range(8)]
         a = {(i, k): row_of(cols[k], i) for k in range(8) for i in range(k, 8)}
         drow = [row_of(D[b], j) for j in range(8)]
-        nrow = [row_of(N[b], j) for j in range(8)]
+        inner = (lane >= 8 * b) & (lane < 8 * b + 8)
+        done = lane < 8 * b + 8
+        left = jnp.where(lane < 8 * b, D[b], jnp.where(lane == sub + 8 * b, 1.0, 0.0))
+        nrow = [row_of(left, j) for j in range(8)]
         r, l, u, n = {}, {}, [], []
         for j in range(8):
             r[j] = lax.rsqrt(a[j, j])
@@ -74,26 +76,24 @@
             for i in range(j + 1, 8):
                 drow[i] = drow[i] - l[i, j] * u[j]
                 nrow[i] = nrow[i] - l[i, j] * n[j]
+        w = [jnp.where(done, n[j], u[j]) for j in range(8)]
         for v in range(b + 1, 16):
             c = [col_of(D[v], 8 * b + k) for k in range(8)]
-            dv, nv = D[v], N[v]
+            dv = jnp.where(inner, 0.0, D[v])
             for j in range(8):
                 lj = c[j] * r[j]
                 for k in range(j + 1, 8):
                     c[k] = c[k] - lj * l[k, j]
                 if v == b + 1:
                     ahead = [ahead[k] - lj * row_of(lj, k) for k in range(8)]
-                dv = dv - lj * u[j]
-                nv = nv - lj * n[j]
-            D[v], N[v] = dv, nv
+                dv = dv - lj * w[j]
+            D[v] = dv
         db, nb = u[0], n[0]
         for j in range(1, 8):
             db = jnp.where(sub == j, u[j], db)
             nb = jnp.where(sub == j, n[j], nb)
-        D[b] = jnp.where(lane >= 8 * b + sub, db, zero)
-        N[b] = nb
-        dref[8 * b : 8 * b + 8, :] = D[b]
-        nref[8 * b : 8 * b + 8, :] = N[b]
+        dref[8 * b : 8 * b + 8, :] = jnp.where(lane >= 8 * b + sub, db, zero)
+        nref[8 * b : 8 * b + 8, :] = nb
 
 
 def fac_kernel(level_no, last, offset, size_rows, pos_ref, t_ref, tail_in, *refs):
@@ -313,20 +313,15 @@
 
 
 def gather_kernel(
-    count, levels, hosted, strip_in, cols_in, vals_in, diag_ref, t_ref, tail_out, *refs
+    count, levels, hosted, strip_in, cols_ref, vals_ref, diag_ref, t_ref, tail_out, *refs
 ):
     packs = refs[:hosted]
     (
-        dense_out, deep_out, land_ref, dense_ref, deep_ref, tail_ref, strip_ref, cols_ref, vals_ref,
+        dense_out, deep_out, land_ref, dense_ref, deep_ref, tail_ref, strip_ref,
         send_sem, recv_sem, out_sem, *leaf_sems,
     ) = refs[hosted:]
-    fetches = [
-        pltpu.make_async_copy(strip_in, strip_ref, out_sem.at[3]),
-        pltpu.make_async_copy(cols_in, cols_ref, out_sem.at[4]),
-        pltpu.make_async_copy(vals_in, vals_ref, out_sem.at[5]),
-    ]
-    for copy in fetches:
-        copy.start()
+    fetch = pltpu.make_async_copy(strip_in, strip_ref, out_sem.at[3])
+    fetch.start()
     leaf = lax.axis_index("leaf")
     me, place, twin_of = ring_of(count)
     rows = strip_ref.shape[0]
@@ -335,7 +330,7 @@
     span = 1 << hosted
     others = [{"leaf": leaf - lax.rem(leaf, span) + lax.rem(leaf + d, span)} for d in range(1, span)]
     greet([ahead, behind, twin] + others)
-    fetches[0].wait()
+    fetch.wait()
 
     def needed(index, c):
         return index * rows // cut >= c
@@ -356,8 +351,6 @@
     each(me, lambda c: move(1, me, c, behind).start())
     each(me, lambda c: move(3, me, c, twin).start())
     land_ref[pl.ds(pl.multiple_of(me * rows, rows), rows), :] = strip_ref[...]
-    for copy in fetches[1:]:
-        copy.wait()
     coupling_rows(me, leaf, count, levels, cols_ref, vals_ref, diag_ref, dense_ref, deep_ref)
     parts = [(leaf, count, n + 1, dense_ref, deep_ref, packs[n], None, leaf_sems[n]) for n in range(hosted)]
     for part in parts:
@@ -414,7 +407,7 @@
             pltpu.HBM((WIDE // count, WIDE), F32),
             pltpu.HBM((8, SEP), F32),
         ],
-        in_specs=[HBM_SPEC] * 3 + [VMEM_SPEC],
+        in_specs=[HBM_SPEC] + [VMEM_SPEC] * 3,
         out_specs=[VMEM_SPEC] + [HBM_SPEC] * (3 + hosted),
         scratch_shapes=[
             pltpu.VMEM((WIDE, WIDE), F32),
@@ -422,17 +415,15 @@
             pltpu.VMEM((8, SEP), F32),
             pltpu.VMEM((BND + 8, BND), F32),
             pltpu.VMEM(strip.shape, F32),
-            pltpu.VMEM(cols.shape, jnp.int32),
-            pltpu.VMEM(vals.shape, F32),
             pltpu.SemaphoreType.DMA((7, CUTS)),
             pltpu.SemaphoreType.DMA((7, CUTS)),
-            pltpu.SemaphoreType.DMA((6,)),
+            pltpu.SemaphoreType.DMA((4,)),
         ]
         + [pltpu.SemaphoreType.DMA((2, 2, 2 << n)) for n in range(hosted)],
         compiler_params=pltpu.CompilerParams(
             collective_id=cid, has_side_effects=True, vmem_limit_bytes=VMEM_LIMIT
         ),
-    )(in_hbm(strip), in_hbm(cols), in_hbm(vals), diag)
+    )(in_hbm(strip), cols, vals, diag)
 
 
 PART = 32

time: 295 us -> 291 us (0.986)
  Pallas kernels: 260 us -> 257 us
    pallas_call x6, Pallas kernels: 116 us -> 111 us  [factor(): pl.pallas_call(functools.partial(fac_kernel, level_no, last, offset, size...]
where the time goes in v2:
time: 291 us; the launch traced here: 288 us
  Pallas kernels  257 us (88%)
  between operations  14.2 us (5%)
  waiting for transfers between devices  10.9 us (4%)
  local copies, waits for them, and re-layouts  4.9 us (2%)
    pallas_call x5, Pallas kernels, swap_assemble(): pl.pallas_call(functools.partial(swap_kernel, count, bit, map_base, hosts...  119 us
    pallas_call x6, Pallas kernels, factor(): pl.pallas_call(functools.partial(fac_kernel, level_no, last, offset, size...  111 us
    pallas_call x1, Pallas kernels, gather_front(): pl.pallas_call(functools.partial(gather_kernel, count, levels, hosted), o...  26.5 us
    all_gather x5, waiting for transfers between devices, body(): lax.all_gather(packs[level_no], 'front', axis=0, axis_index_groups=same_c...  10.1 us
  transfers between devices with their start and end apart: 5, of which 1 were waited for; matrix products, arithmetic and copies ran while one was open for 0% of the time, Pallas kernels for 66%

profile of v2, /device:TPU:1, one launch (start us, length us, event | category | flops | bytes accessed | tf_op | source)
XLA Modules:
  0.0 288.2 jit_solution(4434890253958963983)
XLA Ops:
  7.2 0.8 copy.18
  8.1 0.8 copy.19
  8.9 0.8 copy.12.diag_ref
  9.7 26.5 %shard_map.68 = (f32[512,1024]{1,0:T(8,128)S(1)}, f32[520,512]{1,0:T(8,128)}, f32[192,512]{1,0:T(8,128)}, f32[192,512]{1,0:T(8,128)}, f32[128,1024]{1,0:T(8,128)}, /*index=5*/f32[8,512]{1,0:T(8,128)}) custom-call(f32[128,1024]{1,0:T(8,128)} %bitcast.28, s32[124,128]{1,0:T(8,128)S(1)} %bitcast.21, f32[124,128]{1,0:T(8,128)S(1)} %bitcast.20, ...), custom_call_target="tpu_custom_call" | custom-call | tf_op jit(solution)/shard_map/pallas_call | solution.py:401
  36.2 0.0 all-gather.13.cloned.1.call-start
  36.2 0.7 all-gather.13.cloned.1.call-update
  36.9 0.2 all-gather.15.cloned.1.call-start
  37.2 0.1 stack.27.pos_ref
  37.3 18.7 %shard_map.69 = (f32[252,512]{1,0:T(8,128)}, f32[520,512]{1,0:T(8,128)}) custom-call(s32[6]{0:T(128)S(1)} %stack.27.pos_ref, f32[512,1024]{1,0:T(8,128)S(1)} %get-tuple-element.33.t_ref, f32[520,512]{1,0:T(8,128)} %get-tuple-element.34.tail_in), custom_call_target="tpu_custom_call" | custom-call | tf_op jit(solution)/shard_map/pallas_call | solution.py:168
  56.0 10.0 %all-gather.11.cloned.1.call-done = f32[768,512]{1,0:T(8,128)} async-done(((f32[192,512]{1,0:T(8,128)}), f32[768,512]{1,0:T(8,128)}) %all-gather.11.cloned.1.call-update) | async-done | bytes 1572880 | tf_op jit(solution)/shard_map/all_gather | solution.py:646
  66.0 21.7 %shard_map.70 = (f32[512,1024]{1,0:T(8,128)S(1)}, f32[520,512]{1,0:T(8,128)}, f32[192,512]{1,0:T(8,128)}) custom-call(f32[520,512]{1,0:T(8,128)} %get-tuple-element.35.upd_in, s32[62,512]{1,0:T(8,128)S(1)} %copy-done, f32[4,192,512]{2,1,0:T(8,128)} %bitcast.24, f32[128,1024]{1,0:T(8,128)} %get-tuple-element.37.refs_0_, f32[8,512]{1,0:T(8,128)} %get-tuple-element.38.refs_1_), custom_call_target="tpu_custom_call" | custom-call | tf_op jit(solution)/shard_map/pallas_call | solution.py:614
  87.7 0.3 all-gather.17.cloned.1.call-start
  88.0 18.7 %shard_map.71 = (f32[252,512]{1,0:T(8,128)}, f32[520,512]{1,0:T(8,128)}) custom-call(s32[6]{0:T(128)S(1)} %stack.27.pos_ref, f32[512,1024]{1,0:T(8,128)S(1)} %get-tuple-element.39.t_ref, f32[520,512]{1,0:T(8,128)} %get-tuple-element.40.tail_in, f32[252,512]{1,0:T(8,128)} %get-tuple-element.41.refs_0_), custom_call_target="tpu_custom_call", output_to_operand_aliasing={{0}: (3, {})} | custom-call | tf_op jit(solution)/shard_map/pallas_call | solution.py:168
  106.7 29.4 %shard_map.72 = (f32[512,1024]{1,0:T(8,128)S(1)}, f32[520,512]{1,0:T(8,128)}, f32[192,512]{1,0:T(8,128)}) custom-call(f32[520,512]{1,0:T(8,128)} %get-tuple-element.42.upd_in, s32[62,512]{1,0:T(8,128)S(1)} %copy-done, f32[4,192,512]{2,1,0:T(8,128)} %bitcast.23, f32[128,1024]{1,0:T(8,128)} %get-tuple-element.37.refs_0_, f32[8,512]{1,0:T(8,128)} %get-tuple-element.38.refs_1_), custom_call_target="tpu_custom_call" | custom-call | tf_op jit(solution)/shard_map/pallas_call | solution.py:614
  136.1 0.4 all-gather.19.cloned.1.call-start
  136.6 18.6 %shard_map.73 = (f32[252,512]{1,0:T(8,128)}, f32[520,512]{1,0:T(8,128)}) custom-call(s32[6]{0:T(128)S(1)} %stack.27.pos_ref, f32[512,1024]{1,0:T(8,128)S(1)} %get-tuple-element.44.t_ref, f32[520,512]{1,0:T(8,128)} %get-tuple-element.45.tail_in, f32[252,512]{1,0:T(8,128)} %get-tuple-element.46.refs_0_), custom_call_target="tpu_custom_call", output_to_operand_aliasing={{0}: (3, {})} | custom-call | tf_op jit(solution)/shard_map/pallas_call | solution.py:168
  155.2 24.4 %shard_map.74 = (f32[512,1024]{1,0:T(8,128)S(1)}, f32[520,512]{1,0:T(8,128)}, f32[192,512]{1,0:T(8,128)}) custom-call(f32[520,512]{1,0:T(8,128)} %get-tuple-element.47.upd_in, s32[62,512]{1,0:T(8,128)S(1)} %copy-done, f32[4,192,512]{2,1,0:T(8,128)} %bitcast.25, f32[128,1024]{1,0:T(8,128)} %get-tuple-element.37.refs_0_, f32[8,512]{1,0:T(8,128)} %get-tuple-element.38.refs_1_), custom_call_target="tpu_custom_call" | custom-call | tf_op jit(solution)/shard_map/pallas_call | solution.py:614
  179.6 18.8 %shard_map.75 = (f32[252,512]{1,0:T(8,128)}, f32[520,512]{1,0:T(8,128)}) custom-call(s32[6]{0:T(128)S(1)} %stack.27.pos_ref, f32[512,1024]{1,0:T(8,128)S(1)} %get-tuple-element.49.t_ref, f32[520,512]{1,0:T(8,128)} %get-tuple-element.50.tail_in, f32[252,512]{1,0:T(8,128)} %get-tuple-element.51.refs_0_), custom_call_target="tpu_custom_call", output_to_operand_aliasing={{0}: (3, {})} | custom-call | tf_op jit(solution)/shard_map/pallas_call | solution.py:168
  198.5 21.2 %shard_map.76 = (f32[512,1024]{1,0:T(8,128)S(1)}, f32[520,512]{1,0:T(8,128)}) custom-call(f32[520,512]{1,0:T(8,128)} %get-tuple-element.52.upd_in, s32[62,512]{1,0:T(8,128)S(1)} %copy-done, f32[4,192,512]{2,1,0:T(8,128)} %bitcast.26), custom_call_target="tpu_custom_call" | custom-call | tf_op jit(solution)/shard_map/pallas_call | solution.py:614
  219.7 18.9 %shard_map.77 = (f32[252,512]{1,0:T(8,128)}, f32[520,512]{1,0:T(8,128)}) custom-call(s32[6]{0:T(128)S(1)} %stack.27.pos_ref, f32[512,1024]{1,0:T(8,128)S(1)} %get-tuple-element.54.t_ref, f32[520,512]{1,0:T(8,128)} %get-tuple-element.55.tail_in, f32[252,512]{1,0:T(8,128)} %get-tuple-element.56.refs_0_), custom_call_target="tpu_custom_call", output_to_operand_aliasing={{0}: (3, {})} | custom-call | tf_op jit(solution)/shard_map/pallas_call | solution.py:168
  238.6 22.1 %shard_map.78 = (f32[512,1024]{1,0:T(8,128)S(1)}, f32[520,512]{1,0:T(8,128)}) custom-call(f32[520,512]{1,0:T(8,128)} %get-tuple-element.57.upd_in, s32[62,512]{1,0:T(8,128)S(1)} %copy-done, f32[4,192,512]{2,1,0:T(8,128)} %bitcast.27), custom_call_target="tpu_custom_call" | custom-call | tf_op jit(solution)/shard_map/pallas_call | solution.py:614
  260.7 17.7 %shard_map.79 = (f32[252,512]{1,0:T(8,128)}, f32[8,128]{1,0:T(8,128)S(1)}) custom-call(s32[6]{0:T(128)S(1)} %stack.27.pos_ref, f32[512,1024]{1,0:T(8,128)S(1)} %get-tuple-element.59.t_ref, f32[520,512]{1,0:T(8,128)} %get-tuple-element.60.tail_in, f32[252,512]{1,0:T(8,128)} %get-tuple-element.61.refs_0_), custom_call_target="tpu_custom_call", output_to_operand_aliasing={{0}: (3, {})} | custom-call | tf_op jit(solution)/shard_map/pallas_call | solution.py:168
  278.4 2.4 copy.13
  280.8 0.6 reduce_sum.9
  (11 shorter events, 0.2 us)
Async XLA Ops:
  7.2 58.8 %all-gather.11.cloned.1.call-start = ((), (), s32[]{:S(2)}) async-start(), calls=%async_computation | async-start | bytes 1966080 | tf_op jit(solution)/shard_map/all_gather | solution.py:646
  36.2 70.5 %all-gather.13.cloned.1.call-start = ((), (), s32[]{:S(2)}) async-start(), calls=%async_computation.1 | async-start | bytes 1966080 | tf_op jit(solution)/shard_map/all_gather | solution.py:646
  36.9 118.3 %all-gather.15.cloned.1.call-start = ((), (), s32[]{:S(2)}) async-start(), calls=%async_computation.2 | async-start | bytes 1966080 | tf_op jit(solution)/shard_map/all_gather | solution.py:646
  37.3 28.7 %copy-start = (s32[62,512]{1,0:T(8,128)S(1)}, s32[62,512]{1,0:T(8,128)}, u32[]{:S(2)}) copy-start(s32[62,512]{1,0:T(8,128)} %maps_ref.9) | copy-start | bytes 380932
  87.7 110.8 %all-gather.17.cloned.1.call-start = ((), (), s32[]{:S(2)}) async-start(), calls=%async_computation.3 | async-start | bytes 1966080 | tf_op jit(solution)/shard_map/all_gather | solution.py:646
  136.1 102.4 %all-gather.19.cloned.1.call-start = ((), (), s32[]{:S(2)}) async-start(), calls=%async_computation.4 | async-start | bytes 1966080 | tf_op jit(solution)/shard_map/all_gather | solution.py:646
Sparse Core Ops, SparseCore 0:
  36.3 29.6 all-gather.10
  67.8 29.1 all-gather.12
  98.8 31.6 all-gather.14
  136.2 24.1 all-gather.16
  179.8 27.5 all-gather.18
